TPU v7x, 32 devices: a whole 2x2x4 slice. The times are simulated.
32 devices in a mesh: seq: 16 (over z, y, x), doc: 2 (over core).
Axes of the slice: x: 2, y: 2, z: 4, core: 2. Of those that a mesh axis runs over, the one named last changes fastest.
Arguments:
- conv_input: bfloat16 [4096, 4352], P(('doc', 'seq')), parts along dimension 0, may hold values from -6 to 6
- gate_input: bfloat16 [4096, 4096], P(('doc', 'seq')), parts along dimension 0, may hold values from -6 to 6
- step_input: bfloat16 [4096, 64], P(('doc', 'seq')), parts along dimension 0, may hold values from -1.1 to 2.9
- conv_weight: float32 [4, 4352], replicated, may hold values from -3 to 3
- convolution_bias: float32 [4352], replicated, may hold values from -0.5 to 0.5
- step_bias: float32 [64], replicated, may hold values from -12 to -2, as said below
- decay_log: float32 [64], replicated, may hold values from -3.3 to -1, as said below
- skip_gain: float32 [64], replicated, may hold values from 0.5 to 2
- norm_gain: float32 [4096], replicated, may hold values from 0.5 to 1.5
Outputs:
- normed: bfloat16 [4096, 4096], P(('doc', 'seq')), parts along dimension 0
There are 2 independent parts, one for each index of `doc`. A program takes and returns all parts, laid end to end along the dimension named above; an argument that names none is the same for every part. Nothing has to cross between parts.
Inputs may be any that keep to these rules, and one draw needn't show every extreme that they name: `decay_log`: one value a head. `step_bias`: one value a head.
All inputs are finite; a program needn't handle non-finite values.
Results may differ from a plain program's by a relative error of at most 0.0051.
Values may be sent and summed in bfloat16 or wider, within the bound.
A program may use at most 64 MiB of HBM per device.

v0:
```python
import jax
import jax.numpy as jnp
from jax import lax
from jax.sharding import PartitionSpec as P

HEADDIM = 64
STATE = 128
HEADS = 64
STRETCH = 256


def shifted(value, axis, steps):
    count = lax.axis_size(axis)
    initial, last = (max(0, -steps), min(count, count - steps))
    return lax.ppermute(value, axis, [(source, source + steps) for source in range(initial, last)])


def gated_norm(mixed_out, gate_input, norm_gain):
    gated = mixed_out.astype(jnp.float32) * jax.nn.silu(gate_input.astype(jnp.float32))
    spread = jnp.mean(gated * gated, axis=-1, keepdims=True)
    return (gated * lax.rsqrt(spread + 1e-05) * norm_gain[None, :]).astype(jnp.bfloat16)


def convolve(conv_input, conv_weight, convolution_bias):
    tap_count = conv_weight.shape[0]
    row_count = conv_input.shape[0]
    earlier = shifted(conv_input[row_count - (tap_count - 1) :], "seq", 1)
    padded = jnp.concatenate([earlier, conv_input], axis=0).astype(jnp.float32)
    mixed = convolution_bias[None, :]
    for offset in range(tap_count):
        mixed = mixed + conv_weight[offset][None, :] * padded[offset : offset + row_count]
    return jax.nn.silu(mixed).astype(jnp.bfloat16)


def dual_form(values, step_size, decay_rate, b_rows, c_rows, block_len):
    highest = lax.Precision.HIGHEST
    row_count, head_count, head_width = values.shape
    state_width = b_rows.shape[1]
    blocks = row_count // block_len
    block_values = values.reshape(blocks, block_len, head_count, head_width)
    block_step_sizes = step_size.reshape(blocks, block_len, head_count)
    block_b = b_rows.reshape(blocks, block_len, state_width)
    block_c = c_rows.reshape(blocks, block_len, state_width)
    within = jnp.cumsum(block_step_sizes * decay_rate[None, None, :], axis=1)
    ends = within[:, -1, :]
    totals = jnp.cumsum(ends, axis=0)
    before = totals - ends
    lower = jnp.arange(block_len)[:, None] >= jnp.arange(block_len)[None, :]
    turned = jnp.transpose(within, (0, 2, 1))
    diffs = jnp.where(lower[None, None], turned[:, :, :, None] - turned[:, :, None, :], -jnp.inf)
    scores = jnp.einsum("ctn,csn->cts", block_c, block_b, precision=highest)
    mixing = (
        jnp.exp(diffs) * scores[:, None] * jnp.transpose(block_step_sizes, (0, 2, 1))[:, :, None, :]
    )
    inside = jnp.einsum("chts,cshp->cthp", mixing, block_values, precision=highest)
    tail = jnp.exp(ends[:, None, :] - within) * block_step_sizes
    weighted = tail[:, :, :, None] * block_values
    states = jnp.einsum("cshp,csn->chpn", weighted, block_b, precision=highest)
    order = jnp.arange(blocks)
    earlier_mask = order[:, None] > order[None, :]
    gap = jnp.where(earlier_mask[None], before.T[:, :, None] - totals.T[:, None, :], -jnp.inf)
    entering = jnp.einsum("hcd,dhpn->chpn", jnp.exp(gap), states, precision=highest)
    outside = jnp.exp(within)[:, :, :, None] * jnp.einsum(
        "ctn,chpn->cthp", block_c, entering, precision=highest
    )
    result = (inside + outside).reshape(row_count, head_count, head_width)
    last = totals[-1]
    final = jnp.einsum("dh,dhpn->hpn", jnp.exp(last[None, :] - totals), states, precision=highest)
    decay_sum = (before[:, None, :] + within).reshape(row_count, head_count)
    return (result, final, decay_sum, last)


def shards(
    conv_input,
    gate_input,
    step_input,
    conv_weight,
    convolution_bias,
    step_bias,
    decay_log,
    skip_gain,
    norm_gain,
):
    inner_width = HEADS * HEADDIM
    decay_rate = -jnp.exp(decay_log)
    activated = convolve(conv_input, conv_weight, convolution_bias)
    head_values, head_steps = (
        lax.all_to_all(activated[:, :inner_width], "seq", split_axis=1, concat_axis=0, tiled=True),
        lax.all_to_all(step_input, "seq", split_axis=1, concat_axis=0, tiled=True),
    )
    shared = lax.all_gather(activated[:, inner_width:], "seq", axis=0, tiled=True)
    full_rows = shared.shape[0]
    own_heads = head_steps.shape[1]
    first_head = lax.axis_index("seq") * own_heads
    own_bias = lax.dynamic_slice_in_dim(step_bias, first_head, own_heads)
    own_rate = lax.dynamic_slice_in_dim(decay_rate, first_head, own_heads)
    own_skip = lax.dynamic_slice_in_dim(skip_gain, first_head, own_heads)
    values = head_values.astype(jnp.float32).reshape(full_rows, own_heads, HEADDIM)
    shared_rows = shared.astype(jnp.float32)
    step_size = jax.nn.softplus(head_steps.astype(jnp.float32) + own_bias[None, :])
    result, final, decay_sum, last = dual_form(
        values,
        step_size,
        own_rate,
        shared_rows[:, :STATE],
        shared_rows[:, STATE:],
        min(STRETCH, full_rows),
    )
    result = result + own_skip[None, :, None] * values
    head_output = result.astype(jnp.bfloat16).reshape(full_rows, own_heads * HEADDIM)
    mixed_out = lax.all_to_all(head_output, "seq", split_axis=0, concat_axis=1, tiled=True)
    return gated_norm(mixed_out, gate_input, norm_gain)


def solution(mesh):
    in_specs = (
        P(("doc", "seq"), None),
        P(("doc", "seq"), None),
        P(("doc", "seq"), None),
        P(),
        P(),
        P(),
        P(),
        P(),
        P(),
    )
    out_specs = P(("doc", "seq"), None)
    return jax.shard_map(shards, mesh=mesh, in_specs=in_specs, out_specs=out_specs, check_vma=False)
```

profile of v0, /device:TPU:0, one launch (start us, length us, event | category | flops | bytes accessed | tf_op | source)
XLA Modules:
  0.0 146.6 jit_solution(9924083408817625690)
XLA Ops:
  6.5 8.4 %all-to-all-start.1 = ((bf16[128,16,4]{0,2,1:T(4,128)(2,1)}), bf16[128,16,4]{0,2,1:T(4,128)(2,1)S(1)}, u32[]{:S(2)}, u32[]{:S(2)}) async-start(bf16[128,16,4]{0,2,1:T(4,128)(2,1)} %bitcast.77), calls=%async_computation.1 | async-start | bytes 32768 | tf_op jit(solution)/shard_map/all_to_all | solution.py:89
  15.0 0.9 slice.49
  15.9 3.8 %collective-permute-start = (bf16[3,4352]{1,0:T(4,128)(2,1)S(1)}, bf16[3,4352]{1,0:T(4,128)(2,1)S(1)}, u32[]{:S(2)}, u32[]{:S(2)}) collective-permute-start(bf16[3,4352]{1,0:T(4,128)(2,1)S(1)} %slice.49), channel_id=1, source_target_pairs={{0,2},{2,4},{4,6},{6,8},{8,10},{10,12},{12,14},{14,16},{16,18},{18... | collective-permute-start | bytes 78344 | tf_op jit(solution)/shard_map/ppermute | solution.py:15
  19.8 1.2 slice_reduce_fusion.4
  21.0 1.7 %copy.46 = bf16[128,4352]{0,1:T(8,128)(2,1)S(1)} copy(bf16[128,4352]{1,0:T(8,128)(2,1)} %param.9) | data formatting | bytes 2228224 | tf_op args[0]
  24.2 5.5 %multiply_convert_fusion = bf16[128,4352]{0,1:T(8,128)(2,1)S(1)} fusion(f32[131,4352]{0,1:T(8,128)S(1)} %maximum_convert_fusion, f32[4352]{0:T(1024)S(1)} %get-tuple-element.7, f32[4352]{0:T(1024)S(1)} %get-tuple-element.8, f32[4352]{0:T(1024)S(1)} %get-tuple-element.6, f32[4352]{0:T(1024)S(1)} %get-tuple-element.5, f32[4352]{0:T(1024)S(1)} %copy-done.1), kind=kLoop, calls=%fused_computation.23 | loop fusion | flops 7241728 | bytes 10114048 | tf_op jit(solution)/shard_map/convert_element_type | solution.py:32
  29.7 1.0 slice.68
  31.4 5.9 %all-to-all-start = ((bf16[128,16,256]{0,2,1:T(8,128)(2,1)}), bf16[128,16,256]{0,2,1:T(8,128)(2,1)S(1)}, u32[]{:S(2)}, u32[]{:S(2)}) async-start(bf16[128,16,256]{0,2,1:T(8,128)(2,1)} %bitcast), calls=%async_computation | async-start | bytes 2097152 | tf_op jit(solution)/shard_map/all_to_all | solution.py:88
  37.8 2.3 %reduce-window.6 = f32[8,4,2,128]{3,0,1,2:T(8,128)S(1)} reduce-window(f32[8,4,2,128]{3,0,1,2:T(8,128)S(1)} %copy.49, f32[]{:T(128)} %constant.30.clone.1), window={size=1x1x1x128 pad=0_0x0_0x0_0x127_0}, to_apply=%region_0.1 | reduce-window | flops 1040384 | bytes 65540 | tf_op jit(solution)/shard_map/reduce-window
  40.9 21.0 %all-to-all-done = bf16[128,16,256]{0,2,1:T(8,128)(2,1)S(1)} async-done(((bf16[128,16,256]{0,2,1:T(8,128)(2,1)}), bf16[128,16,256]{0,2,1:T(8,128)(2,1)S(1)}, u32[]{:S(2)}, u32[]{:S(2)}) %all-to-all-start) | async-done | bytes 1048608 | tf_op jit(solution)/shard_map/all_to_all | solution.py:88
  63.2 24.1 %all-gather.2.cloned.1.call-done = bf16[2048,256]{0,1:T(8,128)(2,1)} async-done(((bf16[128,256]{0,1:T(8,128)(2,1)}), bf16[2048,256]{0,1:T(8,128)(2,1)}) %all-gather.2.cloned.1.call-update) | async-done | bytes 1048592 | tf_op jit(solution)/shard_map/all_gather | solution.py:91
  87.2 2.1 %fusion.41 = (bf16[2048,128]{0,1:T(8,128)(2,1)S(1)}, bf16[2048,128]{0,1:T(8,128)(2,1)}) fusion(bf16[2048,256]{0,1:T(8,128)(2,1)} %all-gather.2.cloned.1.call-done), kind=kLoop, calls=%fused_computation.71 | loop fusion | bytes 2097152 | tf_op jit(solution)/shard_map/slice | solution.py:105
  89.6 1.3 copy.53
  91.1 1.6 %fusion.21 = f32[8,4,64,128]{3,2,1,0:T(8,128)S(1)} fusion(bf16[8,256,128,1]{2,1,3,0:T(8,128)(2,1)S(1)} %bitcast.72, f32[8,256,4,64]{1,0,3,2:T(8,128)S(1)} %convert_multiply_fusion.1), kind=kOutput, calls=%fused_computation.31 | convolution fusion | flops 805306368 | bytes 3670016 | tf_op jit(solution)/shard_map/cshp,csn->chpn/dot_general | solution.py:58
  92.8 1.6 %convolution_bitcast_fusion = f32[8,4,64,128]{3,0,2,1:T(8,128)S(1)} fusion(f32[8,4,64,128]{3,2,1,0:T(8,128)S(1)} %fusion.21, f32[4,8]{1,0:T(4,128)S(1)} %bitcast.76, f32[4,8]{1,0:T(4,128)S(1)} %subtract_bitcast_fusion, pred[8,8]{1,0:T(8,128)(4,1)S(1)} %iota_compare_fusion.1), kind=kOutput, calls=%fused_computation.36 | convolution fusion | flops 25166336 | bytes 2097472 | tf_op jit(solution)/shard_map/hcd,dhpn->chpn/dot_general | solution.py:62
  94.4 1.0 fusion.25
  95.8 6.2 %bitcast_add_fusion = f32[8,256,4,64]{1,3,2,0:T(8,128)S(1)} fusion(f32[8,256,4,64]{1,3,2,0:T(8,128)S(1)} %fusion.25, f32[8,4,256]{2,1,0:T(4,128)S(1)} %copy.55, f32[8,256,256]{2,1,0:T(8,128)S(1)} %fusion.43, f32[8,4,256]{2,1,0:T(4,128)S(1)} %copy.51, pred[256,256]{1,0:T(8,128)(4,1)S(1)} %iota_compare_fusion, ...), kind=kOutput, calls=%fused_computation.28 | convolution fusion | flops 1620049920 | bytes 7503872 | tf_op jit(solution)/shard_map/chts,cshp->cthp/dot_general | solution.py:55
  102.0 2.8 %copy.61 = f32[8,256,4,64]{1,0,3,2:T(8,128)} copy(f32[8,256,4,64]{1,3,2,0:T(8,128)S(1)} %bitcast_add_fusion) | data formatting | bytes 4194304 | tf_op jit(solution)/shard_map/add | solution.py:66
  104.8 1.6 %reshape.121 = f32[16,128,256]{1,0,2:T(8,128)S(1)} reshape(f32[8,256,4,64]{1,0,3,2:T(8,128)} %copy.61) | data formatting | bytes 4194304 | tf_op jit(solution)/shard_map/reshape | solution.py:66
  106.4 1.7 %fusion.20 = bf16[16,128,256]{1,2,0:T(8,128)(2,1)} fusion(f32[16,128,256]{1,0,2:T(8,128)S(1)} %reshape.121, f32[256]{0:T(256)S(1)} %mul.156, bf16[128,16,256]{0,2,1:T(8,128)(2,1)S(1)} %all-to-all-done), kind=kLoop, calls=%fused_computation.30 | loop fusion | flops 2097152 | bytes 4195328 | tf_op jit(solution)/shard_map/convert_element_type | solution.py:110
  108.1 4.6 %all-to-all-start.2 = ((bf16[16,128,256]{1,2,0:T(8,128)(2,1)}), bf16[16,128,256]{1,2,0:T(8,128)(2,1)S(1)}, u32[]{:S(2)}, u32[]{:S(2)}) async-start(bf16[16,128,256]{1,2,0:T(8,128)(2,1)} %fusion.20), calls=%async_computation.2 | async-start | bytes 2097152 | tf_op jit(solution)/shard_map/all_to_all | solution.py:111
  113.4 23.4 %all-to-all-done.2 = bf16[16,128,256]{1,2,0:T(8,128)(2,1)S(1)} async-done(((bf16[16,128,256]{1,2,0:T(8,128)(2,1)}), bf16[16,128,256]{1,2,0:T(8,128)(2,1)S(1)}, u32[]{:S(2)}, u32[]{:S(2)}) %all-to-all-start.2) | async-done | bytes 1048608 | tf_op jit(solution)/shard_map/all_to_all | solution.py:111
  137.5 0.9 multiply_convert_fusion.1
  138.4 1.3 copy.64
  (51 shorter events, 6.9 us)
Async XLA Ops:
  6.5 16.2 %copy-start.3 = (f32[64]{0:T(128)S(1)}, f32[64]{0:T(128)}, u32[]{:S(2)}) copy-start(f32[64]{0:T(128)} %param.14) | copy-start | bytes 772
  6.5 24.9 %all-to-all-start.1 = ((bf16[128,16,4]{0,2,1:T(4,128)(2,1)}), bf16[128,16,4]{0,2,1:T(4,128)(2,1)S(1)}, u32[]{:S(2)}, u32[]{:S(2)}) async-start(bf16[128,16,4]{0,2,1:T(4,128)(2,1)} %bitcast.77), calls=%async_computation.1 | async-start | bytes 32768 | tf_op jit(solution)/shard_map/all_to_all | solution.py:89
  15.0 72.3 %all-gather.2.cloned.1.call-start = ((), (), s32[]{:S(2)}) async-start(), calls=%async_computation.3 | async-start | bytes 1114112 | tf_op jit(solution)/shard_map/all_gather | solution.py:91
  15.9 6.9 %collective-permute-start = (bf16[3,4352]{1,0:T(4,128)(2,1)S(1)}, bf16[3,4352]{1,0:T(4,128)(2,1)S(1)}, u32[]{:S(2)}, u32[]{:S(2)}) collective-permute-start(bf16[3,4352]{1,0:T(4,128)(2,1)S(1)} %slice.49), channel_id=1, source_target_pairs={{0,2},{2,4},{4,6},{6,8},{8,10},{10,12},{12,14},{14,16},{16,18},{18... | collective-permute-start | bytes 78344 | tf_op jit(solution)/shard_map/ppermute | solution.py:15
  23.3 0.8 copy-start.1
  29.7 7.6 %copy-start.4 = (f32[64]{0:T(128)S(1)}, f32[64]{0:T(128)}, u32[]{:S(2)}) copy-start(f32[64]{0:T(128)} %param.15) | copy-start | bytes 772
  29.7 7.7 %copy-start.5 = (f32[64]{0:T(128)S(1)}, f32[64]{0:T(128)}, u32[]{:S(2)}) copy-start(f32[64]{0:T(128)} %param.16) | copy-start | bytes 772
  31.4 30.5 %all-to-all-start = ((bf16[128,16,256]{0,2,1:T(8,128)(2,1)}), bf16[128,16,256]{0,2,1:T(8,128)(2,1)S(1)}, u32[]{:S(2)}, u32[]{:S(2)}) async-start(bf16[128,16,256]{0,2,1:T(8,128)(2,1)} %bitcast), calls=%async_computation | async-start | bytes 2097152 | tf_op jit(solution)/shard_map/all_to_all | solution.py:88
  108.1 4.6 %copy-start = (bf16[128,4096]{1,0:T(8,128)(2,1)S(1)}, bf16[128,4096]{1,0:T(8,128)(2,1)}, u32[]{:S(2)}) copy-start(bf16[128,4096]{1,0:T(8,128)(2,1)} %param.10) | copy-start | bytes 3145732
  108.1 28.7 %all-to-all-start.2 = ((bf16[16,128,256]{1,2,0:T(8,128)(2,1)}), bf16[16,128,256]{1,2,0:T(8,128)(2,1)S(1)}, u32[]{:S(2)}, u32[]{:S(2)}) async-start(bf16[16,128,256]{1,2,0:T(8,128)(2,1)} %fusion.20), calls=%async_computation.2 | async-start | bytes 2097152 | tf_op jit(solution)/shard_map/all_to_all | solution.py:111
  112.8 24.8 %copy-start.2 = (f32[4096]{0:T(1024)S(1)}, f32[4096]{0:T(1024)}, u32[]{:S(2)}) copy-start(f32[4096]{0:T(1024)} %param.17) | copy-start | bytes 49156
Sparse Core Ops, SparseCore 0:
  31.5 55.6 all-gather.1
where the time goes:
time: 147 us
  waiting for transfers between devices  68.4 us (47%)
  starting transfers between devices  22.8 us (16%)
  local copies, waits for them, and re-layouts  18.1 us (12%)
  between operations  13.7 us (9%)
  other arithmetic  12.6 us (9%)
  matrix products  10.8 us (7%)
    all_gather x1, waiting for transfers between devices, shards(): lax.all_gather(activated[:, inner_width:], 'seq', axis=0, tiled=True)  24.1 us
    all_to_all x1, waiting for transfers between devices, shards(): lax.all_to_all(head_output, 'seq', split_axis=0, concat_axis=1, tiled=True)  23.4 us
    all_to_all x1, waiting for transfers between devices, shards(): lax.all_to_all(activated[:, :inner_width], 'seq', split_axis=1, concat_ax...  21 us
    all_to_all x1, starting transfers between devices, shards(): lax.all_to_all(step_input, 'seq', split_axis=1, concat_axis=0, tiled=True)  8.44 us
    dot_general x1, matrix products, dual_form(): jnp.einsum('chts,cshp->cthp', mixing, block_values, precision=highest)  6.18 us
    all_to_all x1, starting transfers between devices, shards(): lax.all_to_all(activated[:, :inner_width], 'seq', split_axis=1, concat_ax...  5.89 us
    convert_element_type x1, other arithmetic, convolve(): return jax.nn.silu(mixed).astype(jnp.bfloat16)  5.49 us
    all_to_all x1, starting transfers between devices, shards(): lax.all_to_all(head_output, 'seq', split_axis=0, concat_axis=1, tiled=True)  4.62 us
  transfers between devices with their start and end apart: 5, of which 3 were waited for; matrix products, arithmetic and copies ran while one was open for 12% of the time, Pallas kernels for 0%

commit v1 on v0

--- a/solution.py
+++ b/solution.py
@@ -1,3 +1,4 @@
+import functools
 import jax
 import jax.numpy as jnp
 from jax import lax
@@ -7,6 +8,17 @@
 STATE = 128
 HEADS = 64
 STRETCH = 256
+
+
+def sectors_store(q_in, named_axis):
+    next_value = jnp.split(q_in, lax.psum(1, named_axis), axis=1)
+    d_next = jnp.stack(next_value, axis=0)
+    clean = lax.all_to_all(d_next, named_axis, 0, 0)
+    current_arr = jnp.concatenate(clean, axis=0)
+    return current_arr
+
+
+shape_chains_up = functools.partial(sectors_store, named_axis="seq")
 
 
 def shifted(value, axis, steps):
@@ -85,7 +97,7 @@
     decay_rate = -jnp.exp(decay_log)
     activated = convolve(conv_input, conv_weight, convolution_bias)
     head_values, head_steps = (
-        lax.all_to_all(activated[:, :inner_width], "seq", split_axis=1, concat_axis=0, tiled=True),
+        shape_chains_up(activated[:, :inner_width]),
         lax.all_to_all(step_input, "seq", split_axis=1, concat_axis=0, tiled=True),
     )
     shared = lax.all_gather(activated[:, inner_width:], "seq", axis=0, tiled=True)

time: 147 us -> 167 us (1.14)
  local copies, waits for them, and re-layouts: 18.1 us -> 30.8 us
  waiting for transfers between devices: 68.4 us -> 76 us
    all_gather x1, waiting for transfers between devices: 24.1 us -> 33.3 us  [shards(): lax.all_gather(activated[:, inner_width:], 'seq', axis=0, tiled=True)]
    unnamed x14 -> x28, local copies, waits for them, and re-layouts: 2.37 us -> 11 us
    reshape x1 -> x2, local copies, waits for them, and re-layouts: 1.63 us -> 7.32 us  [dual_form(): result = (inside + outside).reshape(row_count, head_count, head_width)]
    convert_element_type x1, other arithmetic: 5.49 us -> 1.42 us  [convolve(): return jax.nn.silu(mixed).astype(jnp.bfloat16)]
    add x1 -> x0, local copies, waits for them, and re-layouts: 2.79 us -> none  [dual_form(): result = (inside + outside).reshape(row_count, head_count, head_width)]
    all_to_all x1, starting transfers between devices: 8.44 us -> 5.95 us  [shards(): lax.all_to_all(step_input, 'seq', split_axis=1, concat_axis=0, tiled=True)]
    slice x3 -> x1, local copies, waits for them, and re-layouts: 2.51 us -> 0.16 us  [the longest x1 1.31 us: shards(): shared_rows[:, STATE:]]
    convert_element_type x0 -> x1, local copies, waits for them, and re-layouts: none -> 1.91 us  [gated_norm(): mixed_out.astype(jnp.float32) * jax.nn.silu(gate_input.astype(jnp.float32))]
  transfers between devices with their start and end apart: 5 -> 5, of which waited for: 3 -> 3; matrix products, arithmetic and copies ran while one was open for 12% -> 14% of each run, Pallas kernels for 0% -> 0%
where the time goes in v1:
time: 167 us; the launch traced here: 166 us
  waiting for transfers between devices  76 us (46%)
  local copies, waits for them, and re-layouts  30.8 us (18%)
  starting transfers between devices  22.3 us (13%)
  between operations  13.7 us (8%)
  other arithmetic  12.6 us (8%)
  matrix products  10.9 us (7%)
    all_gather x1, waiting for transfers between devices, shards(): lax.all_gather(activated[:, inner_width:], 'seq', axis=0, tiled=True)  33.3 us
    all_to_all x1, waiting for transfers between devices, shards(): lax.all_to_all(head_output, 'seq', split_axis=0, concat_axis=1, tiled=True)  22.6 us
    all_to_all x1, waiting for transfers between devices, sectors_store(): clean = lax.all_to_all(d_next, named_axis, 0, 0)  20.1 us
    unnamed x28, local copies, waits for them, and re-layouts  11 us
    reshape x2, local copies, waits for them, and re-layouts, dual_form(): result = (inside + outside).reshape(row_count, head_count, head_width)  7.32 us
    all_to_all x1, starting transfers between devices, sectors_store(): clean = lax.all_to_all(d_next, named_axis, 0, 0)  6.91 us
    dot_general x1, matrix products, dual_form(): jnp.einsum('chts,cshp->cthp', mixing, block_values, precision=highest)  6.18 us
    all_to_all x1, starting transfers between devices, shards(): lax.all_to_all(step_input, 'seq', split_axis=1, concat_axis=0, tiled=True)  5.95 us
  transfers between devices with their start and end apart: 5, of which 3 were waited for; matrix products, arithmetic and copies ran while one was open for 14% of the time, Pallas kernels for 0%

profile of v1, /device:TPU:0, one launch (start us, length us, event | category | flops | bytes accessed | tf_op | source)
XLA Modules:
  0.0 166.3 jit_solution(6979618665947772171)
XLA Ops:
  7.4 4.8 %collective-permute-start = (bf16[3,4352]{1,0:T(4,128)(2,1)S(1)}, bf16[3,4352]{1,0:T(4,128)(2,1)S(1)}, u32[]{:S(2)}, u32[]{:S(2)}) collective-permute-start(bf16[3,4352]{1,0:T(4,128)(2,1)S(1)} %slice.63), channel_id=1, source_target_pairs={{0,2},{2,4},{4,6},{6,8},{8,10},{10,12},{12,14},{14,16},{16,18},{18... | collective-permute-start | bytes 78344 | tf_op jit(solution)/shard_map/ppermute | solution.py:27
  12.3 6.0 %all-to-all-start.1 = ((bf16[128,16,4]{0,2,1:T(4,128)(2,1)}), bf16[128,16,4]{0,2,1:T(4,128)(2,1)S(1)}, u32[]{:S(2)}, u32[]{:S(2)}) async-start(bf16[128,16,4]{0,2,1:T(4,128)(2,1)} %bitcast.133), calls=%async_computation.1 | async-start | bytes 32768 | tf_op jit(solution)/shard_map/all_to_all | solution.py:101
  18.3 1.2 slice_reduce_fusion.4
  20.2 1.5 maximum_convert_fusion
  21.7 1.4 multiply_convert_fusion
  33.3 6.9 %all-to-all-start = ((bf16[16,128,256]{2,1,0:T(8,128)(2,1)}), bf16[16,128,256]{2,1,0:T(8,128)(2,1)S(1)}, u32[]{:S(2)}, u32[]{:S(2)}) async-start(bf16[16,128,256]{2,1,0:T(8,128)(2,1)} %fusion.28), calls=%async_computation | async-start | bytes 2097152 | tf_op jit(solution)/shard_map/all_to_all | solution.py:16
  41.5 2.5 %reduce-window.6 = f32[8,4,2,128]{3,0,1,2:T(8,128)S(1)} reduce-window(f32[8,4,2,128]{3,0,1,2:T(8,128)S(1)} %copy.63, f32[]{:T(128)} %constant.30.clone.1), window={size=1x1x1x128 pad=0_0x0_0x0_0x127_0}, to_apply=%region_0.1 | reduce-window | flops 1040384 | bytes 65540 | tf_op jit(solution)/shard_map/reduce-window
  44.7 20.1 %all-to-all-done = bf16[16,128,256]{2,1,0:T(8,128)(2,1)S(1)} async-done(((bf16[16,128,256]{2,1,0:T(8,128)(2,1)}), bf16[16,128,256]{2,1,0:T(8,128)(2,1)S(1)}, u32[]{:S(2)}, u32[]{:S(2)}) %all-to-all-start) | async-done | bytes 1048608 | tf_op jit(solution)/shard_map/all_to_all | solution.py:16
  65.9 1.2 reshape_reshape.3
  67.1 1.4 convert_multiply_fusion.1
  68.5 33.3 %all-gather.2.cloned.1.call-done = bf16[2048,256]{1,0:T(8,128)(2,1)} async-done(((bf16[128,256]{1,0:T(8,128)(2,1)}), bf16[2048,256]{1,0:T(8,128)(2,1)}) %all-gather.2.cloned.1.call-update) | async-done | bytes 1048592 | tf_op jit(solution)/shard_map/all_gather | solution.py:103
  101.8 1.3 fusion.56
  103.0 1.7 fusion.20
  104.7 1.6 convolution_bitcast_fusion
  108.5 6.2 %bitcast_add_fusion = f32[8,256,4,64]{1,3,2,0:T(8,128)S(1)} fusion(f32[8,256,4,64]{1,3,2,0:T(8,128)S(1)} %fusion.24, f32[8,4,256]{2,1,0:T(4,128)S(1)} %copy.67, f32[8,256,256]{2,1,0:T(8,128)S(1)} %fusion.58, f32[8,4,256]{2,1,0:T(4,128)S(1)} %copy.65, pred[256,256]{1,0:T(8,128)(4,1)S(1)} %iota_compare_fusion, bf16[8,256,4,64]{1,0,3,2:T(8,128)(2,1)S(1)} %copy-done, ...), kind=kOutput, calls=%fused_computation.27 | convolution fusion | flops 1620049920 | bytes 7503872 | tf_op jit(solution)/shard_map/chts,cshp->cthp/dot_general | solution.py:67
  114.7 3.2 %copy.81 = f32[8,256,4,64]{3,2,1,0:T(4,128)} copy(f32[8,256,4,64]{1,3,2,0:T(8,128)S(1)} %bitcast_add_fusion) | data formatting | bytes 4194304 | tf_op jit(solution)/shard_map/reshape | solution.py:78
  117.9 4.2 %reshape.125 = f32[16,128,256]{2,1,0:T(8,128)S(1)} reshape(f32[8,256,4,64]{3,2,1,0:T(4,128)} %copy.81) | data formatting | bytes 4194304 | tf_op jit(solution)/shard_map/reshape | solution.py:78
  122.0 1.3 add_convert_fusion
  123.3 4.6 %all-to-all-start.2 = ((bf16[16,128,256]{2,1,0:T(8,128)(2,1)}), bf16[16,128,256]{2,1,0:T(8,128)(2,1)S(1)}, u32[]{:S(2)}, u32[]{:S(2)}) async-start(bf16[16,128,256]{2,1,0:T(8,128)(2,1)} %add_convert_fusion), calls=%async_computation.2 | async-start | bytes 2097152 | tf_op jit(solution)/shard_map/all_to_all | solution.py:123
  128.6 22.6 %all-to-all-done.2 = bf16[16,128,256]{2,1,0:T(8,128)(2,1)S(1)} async-done(((bf16[16,128,256]{2,1,0:T(8,128)(2,1)}), bf16[16,128,256]{2,1,0:T(8,128)(2,1)S(1)}, u32[]{:S(2)}, u32[]{:S(2)}) %all-to-all-start.2) | async-done | bytes 1048608 | tf_op jit(solution)/shard_map/all_to_all | solution.py:123
  151.2 1.6 convert_bitcast_fusion
  152.8 1.9 %copy.75 = f32[128,16,256]{0,2,1:T(8,128)S(1)} copy(f32[128,16,256]{2,0,1:T(8,128)} %convert_bitcast_fusion) | data formatting | bytes 4194304 | tf_op jit(solution)/shard_map/convert_element_type | solution.py:31
  155.5 1.7 %multiply_convert_fusion.1 = bf16[128,4096]{0,1:T(8,128)(2,1)} fusion(f32[4096]{0:T(1024)S(1)} %copy-done.3, f32[128]{0:T(128)S(1)} %add_rsqrt_fusion, bf16[128,4096]{0,1:T(8,128)(2,1)S(1)} %copy.76, f32[128,16,256]{0,2,1:T(8,128)S(1)} %copy.75), kind=kLoop, calls=%fused_computation.31 | loop fusion | flops 4718592 | bytes 4211200 | tf_op jit(solution)/shard_map/convert_element_type | solution.py:33
  157.2 2.3 %copy.77 = bf16[128,4096]{1,0:T(8,128)(2,1)} copy(bf16[128,4096]{0,1:T(8,128)(2,1)} %multiply_convert_fusion.1) | data formatting | bytes 2097152 | tf_op jit(solution)/shard_map/convert_element_type | solution.py:33
  (64 shorter events, 18.4 us)
Async XLA Ops:
  6.5 15.2 %copy-start.2 = (f32[4352]{0:T(1024)S(1)}, f32[4352]{0:T(1024)}, u32[]{:S(2)}) copy-start(f32[4352]{0:T(1024)} %param.13) | copy-start | bytes 52228
  7.4 12.8 %collective-permute-start = (bf16[3,4352]{1,0:T(4,128)(2,1)S(1)}, bf16[3,4352]{1,0:T(4,128)(2,1)S(1)}, u32[]{:S(2)}, u32[]{:S(2)}) collective-permute-start(bf16[3,4352]{1,0:T(4,128)(2,1)S(1)} %slice.63), channel_id=1, source_target_pairs={{0,2},{2,4},{4,6},{6,8},{8,10},{10,12},{12,14},{14,16},{16,18},{18... | collective-permute-start | bytes 78344 | tf_op jit(solution)/shard_map/ppermute | solution.py:27
  12.3 21.0 %all-to-all-start.1 = ((bf16[128,16,4]{0,2,1:T(4,128)(2,1)}), bf16[128,16,4]{0,2,1:T(4,128)(2,1)S(1)}, u32[]{:S(2)}, u32[]{:S(2)}) async-start(bf16[128,16,4]{0,2,1:T(4,128)(2,1)} %bitcast.133), calls=%async_computation.1 | async-start | bytes 32768 | tf_op jit(solution)/shard_map/all_to_all | solution.py:101
  23.2 17.1 %copy-start.4 = (f32[64]{0:T(128)S(1)}, f32[64]{0:T(128)}, u32[]{:S(2)}) copy-start(f32[64]{0:T(128)} %param.15) | copy-start | bytes 772
  23.2 17.2 %copy-start.5 = (f32[64]{0:T(128)S(1)}, f32[64]{0:T(128)}, u32[]{:S(2)}) copy-start(f32[64]{0:T(128)} %param.16) | copy-start | bytes 772
  33.3 31.5 %all-to-all-start = ((bf16[16,128,256]{2,1,0:T(8,128)(2,1)}), bf16[16,128,256]{2,1,0:T(8,128)(2,1)S(1)}, u32[]{:S(2)}, u32[]{:S(2)}) async-start(bf16[16,128,256]{2,1,0:T(8,128)(2,1)} %fusion.28), calls=%async_computation | async-start | bytes 2097152 | tf_op jit(solution)/shard_map/all_to_all | solution.py:16
  40.3 61.5 %all-gather.2.cloned.1.call-start = ((), (), s32[]{:S(2)}) async-start(), calls=%async_computation.3 | async-start | bytes 1114112 | tf_op jit(solution)/shard_map/all_gather | solution.py:103
  107.3 1.2 copy-start
  123.3 4.6 %copy-start.1 = (bf16[128,4096]{1,0:T(8,128)(2,1)S(1)}, bf16[128,4096]{1,0:T(8,128)(2,1)}, u32[]{:S(2)}) copy-start(bf16[128,4096]{1,0:T(8,128)(2,1)} %param.10) | copy-start | bytes 3145732
  123.3 27.9 %all-to-all-start.2 = ((bf16[16,128,256]{2,1,0:T(8,128)(2,1)}), bf16[16,128,256]{2,1,0:T(8,128)(2,1)S(1)}, u32[]{:S(2)}, u32[]{:S(2)}) async-start(bf16[16,128,256]{2,1,0:T(8,128)(2,1)} %add_convert_fusion), calls=%async_computation.2 | async-start | bytes 2097152 | tf_op jit(solution)/shard_map/all_to_all | solution.py:123
  154.7 0.8 copy-start.3
Sparse Core Ops, SparseCore 0:
  43.9 57.8 all-gather.1
